TPU v7x, 512 devices: a whole 4x8x8 slice. The times are simulated.
512 devices in a mesh: pot: 128 (over z_lo, y, x, core), grid: 4 (over z_hi).
Axes of the slice: x: 4, y: 8, z: 8 (z_hi: 4, z_lo: 2; z = z_hi * 2 + z_lo), core: 2. Of those that a mesh axis runs over, the one named last changes fastest.
Arguments:
- potentials: float32 [128, 32, 4096], P('pot', 'grid'), may hold values from -24 to 24
- orbitals: bfloat16 [32, 32, 4096], P(None, 'grid', 'pot'), may hold values from -0.5 to 2
- energies: float32 [32], replicated, may hold values from -2 to -0.2
- local_potential: float32 [32, 4096], replicated, may hold values from 0 to 3
- inverse_factor: bfloat16 [128, 128], replicated, may hold values from -8 to 8, as said below
Outputs:
- updated: float32 [128, 32, 4096], P('pot', 'grid')
- margins: float32 [128, 128], P('pot')
Inputs may be any that keep to these rules, and one draw needn't show every extreme that they name: `inverse_factor`: lower triangular with a positive diagonal.
All inputs are finite; a program needn't handle non-finite values.
Results may differ from a plain program's by a relative error of at most 0.0029.
Values may be sent and summed in bfloat16 or wider, within the bound.
A program may use at most 64 MiB of HBM per device.

v0:
```python
import jax
import jax.numpy as jnp
from jax import lax
from jax.sharding import PartitionSpec as P

NX = 64
NY = 64
NZ = 32
ORBITALS = 32
BLOCKS = 4
SWEEPS = 4
DAMPING = 0.8


def padded_2(block, sides, width):
    for axis, dim in sides:
        count = lax.axis_size(axis)
        forward = [(i, i + 1) for i in range(count - 1)]
        backward = [(target, source) for source, target in forward]
        low = lax.ppermute(
            lax.slice_in_dim(block, block.shape[dim] - width, None, axis=dim), axis, forward
        )
        high = lax.ppermute(lax.slice_in_dim(block, 0, width, axis=dim), axis, backward)
        block = jnp.concatenate([low, block, high], axis=dim)
    return block


def plane_neighbours(field, row_width):
    plane_size = field.shape[-1]
    widths = [(0, 0)] * (field.ndim - 1)
    padded = jnp.pad(field, widths + [(row_width, row_width)])
    along_y = padded[..., 2 * row_width :] + padded[..., :plane_size]
    column = jnp.arange(plane_size, dtype=jnp.int32) % row_width
    padded = jnp.pad(field, widths + [(1, 1)])
    right_side = jnp.where(column == row_width - 1, 0.0, padded[..., 2:])
    left_side = jnp.where(column == 0, 0.0, padded[..., :plane_size])
    return along_y + right_side + left_side


def across_slabs(answer):
    padded = padded_2(answer, (("grid", 2),), 1)
    return padded[:, :, 2:] + padded[:, :, :-2]


def absorb(orbital_block, energy_block, fields, local_here, along_planes):
    orbital = orbital_block.astype(jnp.float32)[:, None]
    diagonal = (3.0 + local_here[None] - energy_block[:, None, None])[:, None]
    source = -orbital * fields[None]
    answer = DAMPING * source / diagonal
    for sweep_index in range(SWEEPS - 1):
        nearby = along_planes(answer) + plane_neighbours(answer, NX)
        answer = answer + DAMPING * (source - diagonal * answer + 0.5 * nearby) / diagonal
    return jnp.sum(orbital * answer, axis=0)


def local(potentials, orbitals, energies, local_potential, inverse_factor):
    slab_depth = potentials.shape[1]
    grid_index = lax.axis_index("grid")
    local_here = lax.dynamic_slice_in_dim(local_potential, grid_index * slab_depth, slab_depth, 0)
    block_size = ORBITALS // BLOCKS
    response = jnp.zeros(potentials.shape, jnp.float32)
    for number in range(BLOCKS):
        orbital_block = orbitals[number * block_size : (number + 1) * block_size]
        gathered = lax.all_gather(orbital_block, "pot", axis=2, tiled=True)
        energy_block = energies[number * block_size : (number + 1) * block_size]
        response = response + absorb(gathered, energy_block, potentials, local_here, across_slabs)
    trial_block = (potentials + 4.0 / ORBITALS * response).astype(jnp.bfloat16)
    by_cells = lax.all_to_all(trial_block, "pot", split_axis=2, concat_axis=0, tiled=True)
    row_count = by_cells.shape[0]
    flattened = by_cells.reshape(row_count, -1)
    partial_margins = lax.dot_general(
        flattened, flattened, (((1,), (1,)), ((), ())), preferred_element_type=jnp.float32
    )
    combined = jnp.dot(inverse_factor, flattened, preferred_element_type=jnp.float32).reshape(
        by_cells.shape
    )
    updated = lax.all_to_all(combined, "pot", split_axis=0, concat_axis=2, tiled=True)
    own_count = potentials.shape[0]
    summed_all = lax.psum(partial_margins, ("pot", "grid"))
    own_rows = lax.dynamic_slice_in_dim(summed_all, lax.axis_index("pot") * own_count, own_count, 0)
    margins = own_rows / (NX * NY * NZ)
    return (updated, margins)


def solution(mesh):
    in_specs = (P("pot", "grid", None), P(None, "grid", "pot"), P(), P(), P())
    out_specs = (P("pot", "grid", None), P("pot", None))
    return jax.shard_map(local, mesh=mesh, in_specs=in_specs, out_specs=out_specs, check_vma=False)
```

profile of v0, /device:TPU:1, one launch (start us, length us, event | category | flops | bytes accessed | tf_op | source)
XLA Modules:
  0.0 1255.0 jit_solution(13859245160564547657)
XLA Ops:
  8.1 192.4 %all_gather.12 = bf16[8,8,4096]{1,0,2:T(8,128)(2,1)} all-gather(bf16[8,8,32]{1,0,2:T(8,128)(2,1)S(1)} %copy.397), channel_id=1, replica_groups=mesh['pot'=128,'grid'=4] {'pot'}, dimensions={2}, use_global_device_ids=true | all-gather | bytes 528384 | tf_op jit(solution)/shard_map/all_gather | solution.py:64
  200.4 7.9 copy.321
  208.4 184.1 %all_gather.13 = bf16[8,8,4096]{1,0,2:T(8,128)(2,1)} all-gather(bf16[8,8,32]{1,0,2:T(8,128)(2,1)S(1)} %copy.398), channel_id=1, replica_groups=mesh['pot'=128,'grid'=4] {'pot'}, dimensions={2}, use_global_device_ids=true | all-gather | bytes 528384 | tf_op jit(solution)/shard_map/all_gather | solution.py:64
  392.5 7.9 copy.338
  400.5 185.2 %all_gather.14 = bf16[8,8,4096]{1,0,2:T(8,128)(2,1)} all-gather(bf16[8,8,32]{1,0,2:T(8,128)(2,1)S(1)} %copy.399), channel_id=1, replica_groups=mesh['pot'=128,'grid'=4] {'pot'}, dimensions={2}, use_global_device_ids=true | all-gather | bytes 528384 | tf_op jit(solution)/shard_map/all_gather | solution.py:64
  585.7 7.9 copy.355
  593.7 184.1 %all_gather.15 = bf16[8,8,4096]{1,0,2:T(8,128)(2,1)} all-gather(bf16[8,8,32]{1,0,2:T(8,128)(2,1)S(1)} %copy.400), channel_id=1, replica_groups=mesh['pot'=128,'grid'=4] {'pot'}, dimensions={2}, use_global_device_ids=true | all-gather | bytes 528384 | tf_op jit(solution)/shard_map/all_gather | solution.py:64
  777.8 7.9 copy.372
  788.3 1.3 collective-permute-start.6
  789.7 6.4 collective-permute-start.7
  796.3 1.3 collective-permute-start
  797.6 6.7 collective-permute-start.1
  805.0 1.3 collective-permute-start.12
  806.6 6.1 collective-permute-start.13
  812.8 1.5 collective-permute-start.18
  814.5 1.4 fusion.66
  816.3 6.1 collective-permute-start.19
  822.5 1.3 collective-permute-start.8
  824.0 1.4 fusion.63
  825.8 6.1 collective-permute-start.9
  832.0 1.3 collective-permute-start.2
  833.5 1.4 fusion.69
  835.3 6.1 collective-permute-start.3
  841.5 1.3 collective-permute-start.14
  843.0 1.4 fusion.72
  844.9 6.1 collective-permute-start.15
  851.1 1.3 collective-permute-start.20
  852.6 1.6 fusion.67
  854.5 6.1 collective-permute-start.21
  860.8 11.6 collective-permute-start.10
  872.5 1.6 fusion.64
  874.5 6.1 collective-permute-start.11
  882.2 1.6 fusion.70
  884.2 6.1 collective-permute-start.5
  891.9 1.6 fusion.73
  894.0 6.1 collective-permute-start.17
  901.7 1.5 fusion.16
  903.1 6.1 collective-permute-start.23
  909.5 1.5 fusion.1
  911.3 1.5 fusion.31
  913.1 1.5 fusion.46
  914.6 3.0 copy.392
  918.1 22.4 %reduce.4 = bf16[4096,8]{1,0:T(8,128)(2,1)S(1)} reduce(bf16[4096,1,8]{2,1,0:T(2,128)(2,1)S(1)} %bitcast.279, bf16[]{:T(256)} %broadcast.208), dimensions={1}, to_apply=%bitcast.262.reduce_sub_computation | reduce | bytes 131074
  941.6 21.8 %all_to_all.33 = bf16[128,2,128]{2,1,0:T(2,128)(2,1)S(1)} all-to-all(bf16[128,2,128]{2,1,0:T(2,128)(2,1)S(1)} %reshape.105), channel_id=1, replica_groups=mesh['pot'=128,'grid'=4] {'pot'}, dimensions={0} | all-to-all | bytes 131072 | tf_op jit(solution)/shard_map/all_to_all | solution.py:68
  963.4 2.8 reshape.106
  966.1 1.9 copy.393
  969.7 5.8 all-to-all-start.1
  976.4 267.5 %all-reduce.26.cloned.1.call-done = f32[128,128]{1,0:T(8,128)} async-done(((f32[128,128]{1,0:T(8,128)}), f32[128,128]{1,0:T(8,128)}) %all-reduce.26.cloned.1.call-update) | async-done | bytes 65552 | tf_op jit(solution)/shard_map/psum | solution.py:79
  (118 shorter events, 22.7 us)
Async XLA Ops:
  7.2 961.2 %copy-start = (bf16[128,128]{1,0:T(8,128)(2,1)S(1)}, bf16[128,128]{1,0:T(8,128)(2,1)}, u32[]{:S(2)}) copy-start(bf16[128,128]{1,0:T(8,128)(2,1)} %param.9) | copy-start | bytes 98308
  777.8 7.9 copy-start.2
  777.8 8.9 copy-start.1
  788.3 18.2 %collective-permute-start.6 = (f32[8,1,1,4096]{3,0,2,1:T(8,128)S(1)}, f32[8,1,1,4096]{3,0,2,1:T(8,128)S(1)}, u32[]{:S(2)}, u32[]{:S(2)}) collective-permute-start(f32[8,1,1,4096]{3,0,2,1:T(8,128)S(1)} %copy.339), channel_id=1, source_target_pairs={{1,0},{2,1},{3,2},{5,4},{6,5},{7,6},{9,8},{10,9},{11,10},{13,12},{... | collective-permute-start | bytes 393224 | tf_op jit(solution)/shard_map/ppermute | solution.py:23
  789.7 23.1 %collective-permute-start.7 = (f32[8,1,1,4096]{3,0,2,1:T(8,128)S(1)}, f32[8,1,1,4096]{3,0,2,1:T(8,128)S(1)}, u32[]{:S(2)}, u32[]{:S(2)}) collective-permute-start(f32[8,1,1,4096]{3,0,2,1:T(8,128)S(1)} %copy.341), channel_id=1, source_target_pairs={{0,1},{1,2},{2,3},{4,5},{5,6},{6,7},{8,9},{9,10},{10,11},{12,13},{... | collective-permute-start | bytes 393224 | tf_op jit(solution)/shard_map/ppermute | solution.py:20
  796.3 20.0 %collective-permute-start = (f32[8,1,1,4096]{3,0,2,1:T(8,128)S(1)}, f32[8,1,1,4096]{3,0,2,1:T(8,128)S(1)}, u32[]{:S(2)}, u32[]{:S(2)}) collective-permute-start(f32[8,1,1,4096]{3,0,2,1:T(8,128)S(1)} %copy.322), channel_id=1, source_target_pairs={{1,0},{2,1},{3,2},{5,4},{6,5},{7,6},{9,8},{10,9},{11,10},{13,12},{... | collective-permute-start | bytes 393224 | tf_op jit(solution)/shard_map/ppermute | solution.py:23
  797.6 24.9 %collective-permute-start.1 = (f32[8,1,1,4096]{3,0,2,1:T(8,128)S(1)}, f32[8,1,1,4096]{3,0,2,1:T(8,128)S(1)}, u32[]{:S(2)}, u32[]{:S(2)}) collective-permute-start(f32[8,1,1,4096]{3,0,2,1:T(8,128)S(1)} %copy.324), channel_id=1, source_target_pairs={{0,1},{1,2},{2,3},{4,5},{5,6},{6,7},{8,9},{9,10},{10,11},{12,13},{... | collective-permute-start | bytes 393224 | tf_op jit(solution)/shard_map/ppermute | solution.py:20
  805.0 20.8 %collective-permute-start.12 = (f32[8,1,1,4096]{3,0,2,1:T(8,128)S(1)}, f32[8,1,1,4096]{3,0,2,1:T(8,128)S(1)}, u32[]{:S(2)}, u32[]{:S(2)}) collective-permute-start(f32[8,1,1,4096]{3,0,2,1:T(8,128)S(1)} %copy.356), channel_id=1, source_target_pairs={{1,0},{2,1},{3,2},{5,4},{6,5},{7,6},{9,8},{10,9},{11,10},{13,12},{... | collective-permute-start | bytes 393224 | tf_op jit(solution)/shard_map/ppermute | solution.py:23
  806.6 25.4 %collective-permute-start.13 = (f32[8,1,1,4096]{3,0,2,1:T(8,128)S(1)}, f32[8,1,1,4096]{3,0,2,1:T(8,128)S(1)}, u32[]{:S(2)}, u32[]{:S(2)}) collective-permute-start(f32[8,1,1,4096]{3,0,2,1:T(8,128)S(1)} %copy.358), channel_id=1, source_target_pairs={{0,1},{1,2},{2,3},{4,5},{5,6},{6,7},{8,9},{9,10},{10,11},{12,13},{... | collective-permute-start | bytes 393224 | tf_op jit(solution)/shard_map/ppermute | solution.py:20
  812.8 22.4 %collective-permute-start.18 = (f32[8,1,1,4096]{3,0,2,1:T(8,128)S(1)}, f32[8,1,1,4096]{3,0,2,1:T(8,128)S(1)}, u32[]{:S(2)}, u32[]{:S(2)}) collective-permute-start(f32[8,1,1,4096]{3,0,2,1:T(8,128)S(1)} %copy.373), channel_id=1, source_target_pairs={{1,0},{2,1},{3,2},{5,4},{6,5},{7,6},{9,8},{10,9},{11,10},{13,12},{... | collective-permute-start | bytes 393224 | tf_op jit(solution)/shard_map/ppermute | solution.py:23
  816.3 25.3 %collective-permute-start.19 = (f32[8,1,1,4096]{3,0,2,1:T(8,128)S(1)}, f32[8,1,1,4096]{3,0,2,1:T(8,128)S(1)}, u32[]{:S(2)}, u32[]{:S(2)}) collective-permute-start(f32[8,1,1,4096]{3,0,2,1:T(8,128)S(1)} %copy.375), channel_id=1, source_target_pairs={{0,1},{1,2},{2,3},{4,5},{5,6},{6,7},{8,9},{9,10},{10,11},{12,13},{... | collective-permute-start | bytes 393224 | tf_op jit(solution)/shard_map/ppermute | solution.py:20
  822.5 22.3 %collective-permute-start.8 = (f32[8,1,1,4096]{3,0,2,1:T(8,128)S(1)}, f32[8,1,1,4096]{3,0,2,1:T(8,128)S(1)}, u32[]{:S(2)}, u32[]{:S(2)}) collective-permute-start(f32[8,1,1,4096]{3,0,2,1:T(8,128)S(1)} %copy.344), channel_id=1, source_target_pairs={{1,0},{2,1},{3,2},{5,4},{6,5},{7,6},{9,8},{10,9},{11,10},{13,12},{... | collective-permute-start | bytes 393224 | tf_op jit(solution)/shard_map/ppermute | solution.py:23
  825.8 25.4 %collective-permute-start.9 = (f32[8,1,1,4096]{3,0,2,1:T(8,128)S(1)}, f32[8,1,1,4096]{3,0,2,1:T(8,128)S(1)}, u32[]{:S(2)}, u32[]{:S(2)}) collective-permute-start(f32[8,1,1,4096]{3,0,2,1:T(8,128)S(1)} %copy.346), channel_id=1, source_target_pairs={{0,1},{1,2},{2,3},{4,5},{5,6},{6,7},{8,9},{9,10},{10,11},{12,13},{... | collective-permute-start | bytes 393224 | tf_op jit(solution)/shard_map/ppermute | solution.py:20
  832.0 22.5 %collective-permute-start.2 = (f32[8,1,1,4096]{3,0,2,1:T(8,128)S(1)}, f32[8,1,1,4096]{3,0,2,1:T(8,128)S(1)}, u32[]{:S(2)}, u32[]{:S(2)}) collective-permute-start(f32[8,1,1,4096]{3,0,2,1:T(8,128)S(1)} %copy.327), channel_id=1, source_target_pairs={{1,0},{2,1},{3,2},{5,4},{6,5},{7,6},{9,8},{10,9},{11,10},{13,12},{... | collective-permute-start | bytes 393224 | tf_op jit(solution)/shard_map/ppermute | solution.py:23
  835.3 25.5 %collective-permute-start.3 = (f32[8,1,1,4096]{3,0,2,1:T(8,128)S(1)}, f32[8,1,1,4096]{3,0,2,1:T(8,128)S(1)}, u32[]{:S(2)}, u32[]{:S(2)}) collective-permute-start(f32[8,1,1,4096]{3,0,2,1:T(8,128)S(1)} %copy.329), channel_id=1, source_target_pairs={{0,1},{1,2},{2,3},{4,5},{5,6},{6,7},{8,9},{9,10},{10,11},{12,13},{... | collective-permute-start | bytes 393224 | tf_op jit(solution)/shard_map/ppermute | solution.py:20
  841.5 32.9 %collective-permute-start.14 = (f32[8,1,1,4096]{3,0,2,1:T(8,128)S(1)}, f32[8,1,1,4096]{3,0,2,1:T(8,128)S(1)}, u32[]{:S(2)}, u32[]{:S(2)}) collective-permute-start(f32[8,1,1,4096]{3,0,2,1:T(8,128)S(1)} %copy.361), channel_id=1, source_target_pairs={{1,0},{2,1},{3,2},{5,4},{6,5},{7,6},{9,8},{10,9},{11,10},{13,12},{... | collective-permute-start | bytes 393224 | tf_op jit(solution)/shard_map/ppermute | solution.py:23
  844.9 35.9 %collective-permute-start.15 = (f32[8,1,1,4096]{3,0,2,1:T(8,128)S(1)}, f32[8,1,1,4096]{3,0,2,1:T(8,128)S(1)}, u32[]{:S(2)}, u32[]{:S(2)}) collective-permute-start(f32[8,1,1,4096]{3,0,2,1:T(8,128)S(1)} %copy.363), channel_id=1, source_target_pairs={{0,1},{1,2},{2,3},{4,5},{5,6},{6,7},{8,9},{9,10},{10,11},{12,13},{... | collective-permute-start | bytes 393224 | tf_op jit(solution)/shard_map/ppermute | solution.py:20
  851.1 33.0 %collective-permute-start.20 = (f32[8,1,1,4096]{3,0,2,1:T(8,128)S(1)}, f32[8,1,1,4096]{3,0,2,1:T(8,128)S(1)}, u32[]{:S(2)}, u32[]{:S(2)}) collective-permute-start(f32[8,1,1,4096]{3,0,2,1:T(8,128)S(1)} %copy.378), channel_id=1, source_target_pairs={{1,0},{2,1},{3,2},{5,4},{6,5},{7,6},{9,8},{10,9},{11,10},{13,12},{... | collective-permute-start | bytes 393224 | tf_op jit(solution)/shard_map/ppermute | solution.py:23
  854.5 35.9 %collective-permute-start.21 = (f32[8,1,1,4096]{3,0,2,1:T(8,128)S(1)}, f32[8,1,1,4096]{3,0,2,1:T(8,128)S(1)}, u32[]{:S(2)}, u32[]{:S(2)}) collective-permute-start(f32[8,1,1,4096]{3,0,2,1:T(8,128)S(1)} %copy.380), channel_id=1, source_target_pairs={{0,1},{1,2},{2,3},{4,5},{5,6},{6,7},{8,9},{9,10},{10,11},{12,13},{... | collective-permute-start | bytes 393224 | tf_op jit(solution)/shard_map/ppermute | solution.py:20
  860.8 33.2 %collective-permute-start.10 = (f32[8,1,1,4096]{3,0,2,1:T(8,128)S(1)}, f32[8,1,1,4096]{3,0,2,1:T(8,128)S(1)}, u32[]{:S(2)}, u32[]{:S(2)}) collective-permute-start(f32[8,1,1,4096]{3,0,2,1:T(8,128)S(1)} %copy.349), channel_id=1, source_target_pairs={{1,0},{2,1},{3,2},{5,4},{6,5},{7,6},{9,8},{10,9},{11,10},{13,12},{... | collective-permute-start | bytes 393224 | tf_op jit(solution)/shard_map/ppermute | solution.py:23
  874.5 25.7 %collective-permute-start.11 = (f32[8,1,1,4096]{3,0,2,1:T(8,128)S(1)}, f32[8,1,1,4096]{3,0,2,1:T(8,128)S(1)}, u32[]{:S(2)}, u32[]{:S(2)}) collective-permute-start(f32[8,1,1,4096]{3,0,2,1:T(8,128)S(1)} %copy.351), channel_id=1, source_target_pairs={{0,1},{1,2},{2,3},{4,5},{5,6},{6,7},{8,9},{9,10},{10,11},{12,13},{... | collective-permute-start | bytes 393224 | tf_op jit(solution)/shard_map/ppermute | solution.py:20
  880.7 22.4 %collective-permute-start.4 = (f32[8,1,1,4096]{3,0,2,1:T(8,128)S(1)}, f32[8,1,1,4096]{3,0,2,1:T(8,128)S(1)}, u32[]{:S(2)}, u32[]{:S(2)}) collective-permute-start(f32[8,1,1,4096]{3,0,2,1:T(8,128)S(1)} %copy.332), channel_id=1, source_target_pairs={{1,0},{2,1},{3,2},{5,4},{6,5},{7,6},{9,8},{10,9},{11,10},{13,12},{... | collective-permute-start | bytes 393224 | tf_op jit(solution)/shard_map/ppermute | solution.py:23
  884.2 25.2 %collective-permute-start.5 = (f32[8,1,1,4096]{3,0,2,1:T(8,128)S(1)}, f32[8,1,1,4096]{3,0,2,1:T(8,128)S(1)}, u32[]{:S(2)}, u32[]{:S(2)}) collective-permute-start(f32[8,1,1,4096]{3,0,2,1:T(8,128)S(1)} %copy.334), channel_id=1, source_target_pairs={{0,1},{1,2},{2,3},{4,5},{5,6},{6,7},{8,9},{9,10},{10,11},{12,13},{... | collective-permute-start | bytes 393224 | tf_op jit(solution)/shard_map/ppermute | solution.py:20
  890.4 20.6 %collective-permute-start.16 = (f32[8,1,1,4096]{3,0,2,1:T(8,128)S(1)}, f32[8,1,1,4096]{3,0,2,1:T(8,128)S(1)}, u32[]{:S(2)}, u32[]{:S(2)}) collective-permute-start(f32[8,1,1,4096]{3,0,2,1:T(8,128)S(1)} %copy.366), channel_id=1, source_target_pairs={{1,0},{2,1},{3,2},{5,4},{6,5},{7,6},{9,8},{10,9},{11,10},{13,12},{... | collective-permute-start | bytes 393224 | tf_op jit(solution)/shard_map/ppermute | solution.py:23
  894.0 17.2 %collective-permute-start.17 = (f32[8,1,1,4096]{3,0,2,1:T(8,128)S(1)}, f32[8,1,1,4096]{3,0,2,1:T(8,128)S(1)}, u32[]{:S(2)}, u32[]{:S(2)}) collective-permute-start(f32[8,1,1,4096]{3,0,2,1:T(8,128)S(1)} %copy.368), channel_id=1, source_target_pairs={{0,1},{1,2},{2,3},{4,5},{5,6},{6,7},{8,9},{9,10},{10,11},{12,13},{... | collective-permute-start | bytes 393224 | tf_op jit(solution)/shard_map/ppermute | solution.py:20
  900.2 12.6 %collective-permute-start.22 = (f32[8,1,1,4096]{3,0,2,1:T(8,128)S(1)}, f32[8,1,1,4096]{3,0,2,1:T(8,128)S(1)}, u32[]{:S(2)}, u32[]{:S(2)}) collective-permute-start(f32[8,1,1,4096]{3,0,2,1:T(8,128)S(1)} %copy.383), channel_id=1, source_target_pairs={{1,0},{2,1},{3,2},{5,4},{6,5},{7,6},{9,8},{10,9},{11,10},{13,12},{... | collective-permute-start | bytes 393224 | tf_op jit(solution)/shard_map/ppermute | solution.py:23
  903.1 9.8 collective-permute-start.23
  969.7 275.5 %all-to-all-start.1 = ((f32[128,1,256]{2,1,0:T(1,128)}), f32[128,1,256]{2,1,0:T(1,128)S(1)}, u32[]{:S(2)}, u32[]{:S(2)}) async-start(f32[128,1,256]{2,1,0:T(1,128)} %reshape.107), calls=%async_computation.1 | async-start | bytes 262144 | tf_op jit(solution)/shard_map/all_to_all | solution.py:77
  975.5 268.4 %all-reduce.26.cloned.1.call-start = ((), (), s32[]{:S(2)}) async-start(), calls=%async_computation.2 | async-start | bytes 131072 | tf_op jit(solution)/shard_map/psum | solution.py:79
Sparse Core Ops, SparseCore 0:
  981.3 262.5 all-reduce.25
where the time goes:
time: 1260 us; the launch traced here: 1250 us
  blocking collectives  768 us (61%)
  waiting for transfers between devices  268 us (21%)
  starting transfers between devices  106 us (8%)
  local copies, waits for them, and re-layouts  52.8 us (4%)
  other arithmetic  44.6 us (4%)
  between operations  15.4 us (1%)
    all_gather x4, blocking collectives, local(): gathered = lax.all_gather(orbital_block, 'pot', axis=2, tiled=True)  746 us
    psum x1, waiting for transfers between devices, local(): summed_all = lax.psum(partial_margins, ('pot', 'grid'))  268 us
    ppermute x12, starting transfers between devices, padded_2(): lax.ppermute(lax.slice_in_dim(block, block.shape[dim] - width, None, axis...  74.2 us
    all_gather x4, local copies, waits for them, and re-layouts, local(): gathered = lax.all_gather(orbital_block, 'pot', axis=2, tiled=True)  31.5 us
    ppermute x12, starting transfers between devices, padded_2(): lax.ppermute(lax.slice_in_dim(block, 0, width, axis=dim), axis, backward)  26 us
  transfers between devices with their start and end apart: 26, of which 1 were waited for; matrix products, arithmetic and copies ran while one was open for 2% of the time, Pallas kernels for 0%

commit v1 on v0

--- a/solution.py
+++ b/solution.py
@@ -61,7 +61,9 @@
     response = jnp.zeros(potentials.shape, jnp.float32)
     for number in range(BLOCKS):
         orbital_block = orbitals[number * block_size : (number + 1) * block_size]
-        gathered = lax.all_gather(orbital_block, "pot", axis=2, tiled=True)
+        gathered = jnp.concatenate(
+            lax.all_to_all(jnp.stack([orbital_block] * lax.axis_size("pot")), "pot", 0, 0), axis=2
+        )
         energy_block = energies[number * block_size : (number + 1) * block_size]
         response = response + absorb(gathered, energy_block, potentials, local_here, across_slabs)
     trial_block = (potentials + 4.0 / ORBITALS * response).astype(jnp.bfloat16)

time: 1260 us -> 623 us (0.49)
  blocking collectives: 768 us -> 29.7 us
  waiting for transfers between devices: 268 us -> 300 us
  local copies, waits for them, and re-layouts: 52.8 us -> 77.8 us
  starting transfers between devices: 106 us -> 127 us
  other arithmetic: 44.6 us -> 64.6 us
    all_gather x4 -> x0, blocking collectives: 746 us -> none  [local(): gathered = lax.all_gather(orbital_block, 'pot', axis=2, tiled=True)]
    convert_element_type x0 -> x8, local copies, waits for them, and re-layouts: none -> 36.2 us  [absorb(): orbital = orbital_block.astype(jnp.float32)[:, None]]
    all_to_all x0 -> x4, starting transfers between devices: none -> 34.3 us  [local(): lax.all_to_all(jnp.stack([orbital_block] * lax.axis_size('pot')), 'pot',...]
    all_gather x4 -> x0, local copies, waits for them, and re-layouts: 31.5 us -> none  [local(): gathered = lax.all_gather(orbital_block, 'pot', axis=2, tiled=True)]
    all_to_all x0 -> x4, waiting for transfers between devices: none -> 26.7 us  [local(): lax.all_to_all(jnp.stack([orbital_block] * lax.axis_size('pot')), 'pot',...]
    unnamed x15 -> x31, local copies, waits for them, and re-layouts: 5.86 us -> 27.5 us
  transfers between devices with their start and end apart: 26 -> 30, of which waited for: 1 -> 6; matrix products, arithmetic and copies ran while one was open for 2% -> 14% of each run, Pallas kernels for 0% -> 0%
where the time goes in v1:
time: 623 us; the launch traced here: 615 us
  waiting for transfers between devices  300 us (48%)
  starting transfers between devices  127 us (20%)
  local copies, waits for them, and re-layouts  77.8 us (12%)
  other arithmetic  64.6 us (10%)
  blocking collectives  29.7 us (5%)
  between operations  15 us (2%)
    psum x1, waiting for transfers between devices, local(): summed_all = lax.psum(partial_margins, ('pot', 'grid'))  265 us
    ppermute x12, starting transfers between devices, padded_2(): lax.ppermute(lax.slice_in_dim(block, block.shape[dim] - width, None, axis...  70.9 us
    convert_element_type x8, local copies, waits for them, and re-layouts, absorb(): orbital = orbital_block.astype(jnp.float32)[:, None]  36.2 us
    all_to_all x4, starting transfers between devices, local(): lax.all_to_all(jnp.stack([orbital_block] * lax.axis_size('pot')), 'pot',...  34.3 us
    all_to_all x1, blocking collectives, local(): lax.all_to_all(trial_block, 'pot', split_axis=2, concat_axis=0, tiled=True)  29.7 us
    unnamed x31, local copies, waits for them, and re-layouts  27.5 us
    all_to_all x4, waiting for transfers between devices, local(): lax.all_to_all(jnp.stack([orbital_block] * lax.axis_size('pot')), 'pot',...  26.7 us
    unnamed x1, other arithmetic  22.4 us
  transfers between devices with their start and end apart: 30, of which 6 were waited for; matrix products, arithmetic and copies ran while one was open for 14% of the time, Pallas kernels for 0%

profile of v1, /device:TPU:1, one launch (start us, length us, event | category | flops | bytes accessed | tf_op | source)
XLA Modules:
  0.0 615.1 jit_solution(9735182819439156228)
XLA Ops:
  8.5 2.8 reshape.299
  11.2 14.2 %all-to-all-start.1 = ((bf16[128,2,1024]{2,1,0:T(2,128)(2,1)}), bf16[128,2,1024]{2,1,0:T(2,128)(2,1)S(1)}, u32[]{:S(2)}, u32[]{:S(2)}) async-start(bf16[128,2,1024]{2,1,0:T(2,128)(2,1)} %reshape.299), calls=%async_computation.1 | async-start | bytes 1048576 | tf_op jit(solution)/shard_map/all_to_all | solution.py:65
  26.0 2.7 reshape.293
  29.2 2.8 reshape.295
  32.5 2.8 reshape.297
  36.3 9.7 %all-to-all-done.1 = bf16[128,2,1024]{2,1,0:T(2,128)(2,1)S(1)} async-done(((bf16[128,2,1024]{2,1,0:T(2,128)(2,1)}), bf16[128,2,1024]{2,1,0:T(2,128)(2,1)S(1)}, u32[]{:S(2)}, u32[]{:S(2)}) %all-to-all-start.1) | async-done | bytes 524320 | tf_op jit(solution)/shard_map/all_to_all | solution.py:65
  46.0 5.9 all-to-all-start.3
  53.4 4.4 copy.20
  57.8 3.5 reshape.289
  61.7 10.7 %all-to-all-done.3 = bf16[128,2,1024]{2,1,0:T(2,128)(2,1)S(1)} async-done(((bf16[128,2,1024]{2,1,0:T(2,128)(2,1)}), bf16[128,2,1024]{2,1,0:T(2,128)(2,1)S(1)}, u32[]{:S(2)}, u32[]{:S(2)}) %all-to-all-start.3) | async-done | bytes 524320 | tf_op jit(solution)/shard_map/all_to_all | solution.py:65
  72.4 6.5 %all-to-all-start.2 = ((bf16[128,2,1024]{2,1,0:T(2,128)(2,1)}), bf16[128,2,1024]{2,1,0:T(2,128)(2,1)}, u32[]{:S(2)}, u32[]{:S(2)}) async-start(bf16[128,2,1024]{2,1,0:T(2,128)(2,1)} %reshape.295), calls=%async_computation.2 | async-start | bytes 1048576 | tf_op jit(solution)/shard_map/all_to_all | solution.py:65
  79.8 6.4 %collective-permute-start.7 = (f32[8,1,1,4096]{3,2,0,1:T(1,128)}, f32[8,1,1,4096]{3,2,0,1:T(1,128)}, u32[]{:S(2)}, u32[]{:S(2)}) collective-permute-start(f32[8,1,1,4096]{3,2,0,1:T(1,128)} %get-tuple-element.7), channel_id=1, source_target_pairs={{0,1},{1,2},{2,3},{4,5},{5,6},{6,7},{8,9},{9,10},{10,11},{12,13},{... | collective-permute-start | bytes 393224 | tf_op jit(solution)/shard_map/ppermute | solution.py:20
  87.6 3.0 reshape.294
  90.6 2.4 convert_bitcast_fusion
  93.0 6.2 %all-to-all-done.2 = bf16[128,2,1024]{2,1,0:T(2,128)(2,1)} async-done(((bf16[128,2,1024]{2,1,0:T(2,128)(2,1)}), bf16[128,2,1024]{2,1,0:T(2,128)(2,1)}, u32[]{:S(2)}, u32[]{:S(2)}) %all-to-all-start.2) | async-done | bytes 524320 | tf_op jit(solution)/shard_map/all_to_all | solution.py:65
  99.3 7.7 %all-to-all-start = ((bf16[128,2,1024]{2,1,0:T(2,128)(2,1)}), bf16[128,2,1024]{2,1,0:T(2,128)(2,1)}, u32[]{:S(2)}, u32[]{:S(2)}) async-start(bf16[128,2,1024]{2,1,0:T(2,128)(2,1)} %reshape.297), calls=%async_computation | async-start | bytes 1048576 | tf_op jit(solution)/shard_map/all_to_all | solution.py:65
  107.0 3.0 reshape.296
  110.1 5.6 fusion.16
  117.5 6.8 %collective-permute-start.9 = (f32[8,1,1,4096]{3,2,0,1:T(1,128)}, f32[8,1,1,4096]{3,2,0,1:T(1,128)}, u32[]{:S(2)}, u32[]{:S(2)}) collective-permute-start(f32[8,1,1,4096]{3,2,0,1:T(1,128)} %get-tuple-element.5), channel_id=1, source_target_pairs={{0,1},{1,2},{2,3},{4,5},{5,6},{6,7},{8,9},{9,10},{10,11},{12,13},{... | collective-permute-start | bytes 393224 | tf_op jit(solution)/shard_map/ppermute | solution.py:20
  125.6 2.5 convert_bitcast_fusion.1
  128.1 3.0 reshape.298
  131.1 3.3 collective-permute-done.8
  134.4 5.3 fusion.20
  140.7 3.9 collective-permute-start.11
  146.1 2.5 convert_bitcast_fusion.3
  148.6 4.4 copy.22
  153.0 3.7 reshape.291
  156.7 6.6 %copy.21 = f32[8,8,128,32]{3,2,1,0:T(8,128)} copy(f32[8,8,128,32]{3,1,0,2:T(8,128)} %convert_bitcast_fusion.1) | data formatting | bytes 2097152 | tf_op jit(solution)/shard_map/convert_element_type | solution.py:46
  163.3 3.5 reshape.290
  166.8 6.6 %copy.19 = f32[8,8,128,32]{3,2,1,0:T(8,128)} copy(f32[8,8,128,32]{3,1,0,2:T(8,128)} %convert_bitcast_fusion.3) | data formatting | bytes 2097152 | tf_op jit(solution)/shard_map/convert_element_type | solution.py:46
  173.4 3.5 reshape.288
  176.9 6.3 %fusion.90 = (f32[8,4096]{1,0:T(8,128)S(1)}, f32[8,1,8,4096]{3,2,0,1:T(8,128)S(1)}, f32[8,1,8,4096]{3,2,0,1:T(8,128)S(1)}, f32[8,1,8,4096]{3,2,0,1:T(8,128)S(1)}) fusion(f32[8,1,8,4096]{3,2,0,1:T(8,128)} %copy-done.1, f32[8,1,8,4096]{3,2,0,1:T(8,128)} %copy-done.4, f32[8,1,1,4096]{3,2,0,1:T(1,128)} %collective-permute-done.11, ...), kind=kLoop, calls=%fused_computation.151 | loop fusion | flops 9404416 | bytes 9052288 | tf_op jit(solution)/shard_map/reduce_sum | solution.py:53
  183.4 4.9 collective-permute-start.19
  189.8 5.9 collective-permute-start.13
  197.2 6.1 collective-permute-start.1
  206.4 6.3 %collective-permute-start.21 = (f32[8,1,1,4096]{3,2,0,1:T(1,128)S(1)}, f32[8,1,1,4096]{3,2,0,1:T(1,128)S(1)}, u32[]{:S(2)}, u32[]{:S(2)}) collective-permute-start(f32[8,1,1,4096]{3,2,0,1:T(1,128)S(1)} %get-tuple-element.23), channel_id=1, source_target_pairs={{0,1},{1,2},{2,3},{4,5},{5,6},{6,7},{8,9},{9,10},{10,11},{12,13},{... | collective-permute-start | bytes 393224 | tf_op jit(solution)/shard_map/ppermute | solution.py:20
  215.8 6.1 collective-permute-start.15
  225.0 6.1 collective-permute-start.3
  234.2 6.1 collective-permute-start.23
  243.4 6.1 collective-permute-start.17
  252.6 6.1 collective-permute-start.5
  263.4 4.6 collective-permute-done.4
  269.5 2.8 copy.23
  272.8 22.4 %reduce.4 = bf16[4096,8]{1,0:T(8,128)(2,1)S(1)} reduce(bf16[4096,1,8]{2,1,0:T(2,128)(2,1)S(1)} %bitcast.55, bf16[]{:T(256)} %broadcast.365), dimensions={1}, to_apply=%bitcast.38.reduce_sub_computation | reduce | bytes 131074
  296.3 29.7 %all_to_all.53 = bf16[128,2,128]{2,1,0:T(2,128)(2,1)S(1)} all-to-all(bf16[128,2,128]{2,1,0:T(2,128)(2,1)S(1)} %reshape.301), channel_id=1, replica_groups=mesh['pot'=128,'grid'=4] {'pot'}, dimensions={0} | all-to-all | bytes 131072 | tf_op jit(solution)/shard_map/all_to_all | solution.py:70
  326.0 2.8 reshape.302
  332.3 5.8 all-to-all-start.5
  339.1 265.1 %all-reduce.26.cloned.1.call-done = f32[128,128]{1,0:T(8,128)} async-done(((f32[128,128]{1,0:T(8,128)}), f32[128,128]{1,0:T(8,128)}) %all-reduce.26.cloned.1.call-update) | async-done | bytes 65552 | tf_op jit(solution)/shard_map/psum | solution.py:81
  (104 shorter events, 50.9 us)
Async XLA Ops:
  7.2 323.8 %copy-start = (bf16[128,128]{1,0:T(8,128)(2,1)S(1)}, bf16[128,128]{1,0:T(8,128)(2,1)}, u32[]{:S(2)}) copy-start(bf16[128,128]{1,0:T(8,128)(2,1)} %param.9) | copy-start | bytes 98308
  11.2 34.8 %all-to-all-start.1 = ((bf16[128,2,1024]{2,1,0:T(2,128)(2,1)}), bf16[128,2,1024]{2,1,0:T(2,128)(2,1)S(1)}, u32[]{:S(2)}, u32[]{:S(2)}) async-start(bf16[128,2,1024]{2,1,0:T(2,128)(2,1)} %reshape.299), calls=%async_computation.1 | async-start | bytes 1048576 | tf_op jit(solution)/shard_map/all_to_all | solution.py:65
  32.0 3.3 copy-start.8
  46.0 26.4 %all-to-all-start.3 = ((bf16[128,2,1024]{2,1,0:T(2,128)(2,1)}), bf16[128,2,1024]{2,1,0:T(2,128)(2,1)S(1)}, u32[]{:S(2)}, u32[]{:S(2)}) async-start(bf16[128,2,1024]{2,1,0:T(2,128)(2,1)} %reshape.293), calls=%async_computation.3 | async-start | bytes 1048576 | tf_op jit(solution)/shard_map/all_to_all | solution.py:65
  57.8 3.6 copy-start.2
  61.3 73.0 %copy-start.1 = (f32[8,1,8,4096]{3,2,0,1:T(8,128)}, f32[8,1,8,4096]{3,2,0,1:T(8,128)S(1)}, u32[]{:S(2)}) copy-start(f32[8,1,8,4096]{3,2,0,1:T(8,128)S(1)} %reshape.289) | copy-start | bytes 3145732
  61.7 24.6 %copy-start.5 = (f32[8,1,8,4096]{3,2,0,1:T(8,128)}, f32[8,1,8,4096]{3,2,0,1:T(8,128)S(1)}, u32[]{:S(2)}) copy-start(f32[8,1,8,4096]{3,2,0,1:T(8,128)S(1)} %subtract_divide_fusion.11) | copy-start | bytes 3145732
  72.4 13.9 %copy-start.7 = (bf16[128,2,1024]{2,1,0:T(2,128)(2,1)}, bf16[128,2,1024]{2,1,0:T(2,128)(2,1)S(1)}, u32[]{:S(2)}) copy-start(bf16[128,2,1024]{2,1,0:T(2,128)(2,1)S(1)} %all-to-all-done.3) | copy-start | bytes 1572868
  72.4 26.9 %all-to-all-start.2 = ((bf16[128,2,1024]{2,1,0:T(2,128)(2,1)}), bf16[128,2,1024]{2,1,0:T(2,128)(2,1)}, u32[]{:S(2)}, u32[]{:S(2)}) async-start(bf16[128,2,1024]{2,1,0:T(2,128)(2,1)} %reshape.295), calls=%async_computation.2 | async-start | bytes 1048576 | tf_op jit(solution)/shard_map/all_to_all | solution.py:65
  79.8 30.2 %collective-permute-start.7 = (f32[8,1,1,4096]{3,2,0,1:T(1,128)}, f32[8,1,1,4096]{3,2,0,1:T(1,128)}, u32[]{:S(2)}, u32[]{:S(2)}) collective-permute-start(f32[8,1,1,4096]{3,2,0,1:T(1,128)} %get-tuple-element.7), channel_id=1, source_target_pairs={{0,1},{1,2},{2,3},{4,5},{5,6},{6,7},{8,9},{9,10},{10,11},{12,13},{... | collective-permute-start | bytes 393224 | tf_op jit(solution)/shard_map/ppermute | solution.py:20
  86.3 23.8 %collective-permute-start.6 = (f32[8,1,1,4096]{3,2,0,1:T(1,128)}, f32[8,1,1,4096]{3,2,0,1:T(1,128)}, u32[]{:S(2)}, u32[]{:S(2)}) collective-permute-start(f32[8,1,1,4096]{3,2,0,1:T(1,128)} %get-tuple-element.6), channel_id=1, source_target_pairs={{1,0},{2,1},{3,2},{5,4},{6,5},{7,6},{9,8},{10,9},{11,10},{13,12},{... | collective-permute-start | bytes 393224 | tf_op jit(solution)/shard_map/ppermute | solution.py:23
  99.3 28.8 %all-to-all-start = ((bf16[128,2,1024]{2,1,0:T(2,128)(2,1)}), bf16[128,2,1024]{2,1,0:T(2,128)(2,1)}, u32[]{:S(2)}, u32[]{:S(2)}) async-start(bf16[128,2,1024]{2,1,0:T(2,128)(2,1)} %reshape.297), calls=%async_computation | async-start | bytes 1048576 | tf_op jit(solution)/shard_map/all_to_all | solution.py:65
  115.6 1.0 copy-start.6
  117.5 13.6 %collective-permute-start.9 = (f32[8,1,1,4096]{3,2,0,1:T(1,128)}, f32[8,1,1,4096]{3,2,0,1:T(1,128)}, u32[]{:S(2)}, u32[]{:S(2)}) collective-permute-start(f32[8,1,1,4096]{3,2,0,1:T(1,128)} %get-tuple-element.5), channel_id=1, source_target_pairs={{0,1},{1,2},{2,3},{4,5},{5,6},{6,7},{8,9},{9,10},{10,11},{12,13},{... | collective-permute-start | bytes 393224 | tf_op jit(solution)/shard_map/ppermute | solution.py:20
  124.3 10.1 %collective-permute-start.8 = (f32[8,1,1,4096]{3,2,0,1:T(1,128)}, f32[8,1,1,4096]{3,2,0,1:T(1,128)}, u32[]{:S(2)}, u32[]{:S(2)}) collective-permute-start(f32[8,1,1,4096]{3,2,0,1:T(1,128)} %get-tuple-element.4), channel_id=1, source_target_pairs={{1,0},{2,1},{3,2},{5,4},{6,5},{7,6},{9,8},{10,9},{11,10},{13,12},{... | collective-permute-start | bytes 393224 | tf_op jit(solution)/shard_map/ppermute | solution.py:23
  139.6 9.0 %copy-start.4 = (f32[8,1,8,4096]{3,2,0,1:T(8,128)}, f32[8,1,8,4096]{3,2,0,1:T(8,128)S(1)}, u32[]{:S(2)}) copy-start(f32[8,1,8,4096]{3,2,0,1:T(8,128)S(1)} %fusion.20) | copy-start | bytes 3145732
  140.7 36.2 %collective-permute-start.11 = (f32[8,1,1,4096]{3,2,0,1:T(1,128)}, f32[8,1,1,4096]{3,2,0,1:T(1,128)}, u32[]{:S(2)}, u32[]{:S(2)}) collective-permute-start(f32[8,1,1,4096]{3,2,0,1:T(1,128)} %get-tuple-element.3), channel_id=1, source_target_pairs={{0,1},{1,2},{2,3},{4,5},{5,6},{6,7},{8,9},{9,10},{10,11},{12,13},{... | collective-permute-start | bytes 393224 | tf_op jit(solution)/shard_map/ppermute | solution.py:20
  144.6 4.0 copy-start.3
  144.6 32.3 %collective-permute-start.10 = (f32[8,1,1,4096]{3,2,0,1:T(1,128)}, f32[8,1,1,4096]{3,2,0,1:T(1,128)}, u32[]{:S(2)}, u32[]{:S(2)}) collective-permute-start(f32[8,1,1,4096]{3,2,0,1:T(1,128)} %get-tuple-element.2), channel_id=1, source_target_pairs={{1,0},{2,1},{3,2},{5,4},{6,5},{7,6},{9,8},{10,9},{11,10},{13,12},{... | collective-permute-start | bytes 393224 | tf_op jit(solution)/shard_map/ppermute | solution.py:23
  183.4 20.0 %collective-permute-start.19 = (f32[8,1,1,4096]{3,2,0,1:T(1,128)S(1)}, f32[8,1,1,4096]{3,2,0,1:T(1,128)S(1)}, u32[]{:S(2)}, u32[]{:S(2)}) collective-permute-start(f32[8,1,1,4096]{3,2,0,1:T(1,128)S(1)} %get-tuple-element.25), channel_id=1, source_target_pairs={{0,1},{1,2},{2,3},{4,5},{5,6},{6,7},{8,9},{9,10},{10,11},{12,13},{... | collective-permute-start | bytes 393224 | tf_op jit(solution)/shard_map/ppermute | solution.py:20
  188.3 16.4 %collective-permute-start.18 = (f32[8,1,1,4096]{3,2,0,1:T(1,128)S(1)}, f32[8,1,1,4096]{3,2,0,1:T(1,128)S(1)}, u32[]{:S(2)}, u32[]{:S(2)}) collective-permute-start(f32[8,1,1,4096]{3,2,0,1:T(1,128)S(1)} %get-tuple-element.24), channel_id=1, source_target_pairs={{1,0},{2,1},{3,2},{5,4},{6,5},{7,6},{9,8},{10,9},{11,10},{13,12},{... | collective-permute-start | bytes 393224 | tf_op jit(solution)/shard_map/ppermute | solution.py:23
  189.8 23.0 %collective-permute-start.13 = (f32[8,1,1,4096]{3,2,0,1:T(1,128)S(1)}, f32[8,1,1,4096]{3,2,0,1:T(1,128)S(1)}, u32[]{:S(2)}, u32[]{:S(2)}) collective-permute-start(f32[8,1,1,4096]{3,2,0,1:T(1,128)S(1)} %get-tuple-element.19), channel_id=1, source_target_pairs={{0,1},{1,2},{2,3},{4,5},{5,6},{6,7},{8,9},{9,10},{10,11},{12,13},{... | collective-permute-start | bytes 393224 | tf_op jit(solution)/shard_map/ppermute | solution.py:20
  195.7 18.3 %collective-permute-start.12 = (f32[8,1,1,4096]{3,2,0,1:T(1,128)S(1)}, f32[8,1,1,4096]{3,2,0,1:T(1,128)S(1)}, u32[]{:S(2)}, u32[]{:S(2)}) collective-permute-start(f32[8,1,1,4096]{3,2,0,1:T(1,128)S(1)} %get-tuple-element.18), channel_id=1, source_target_pairs={{1,0},{2,1},{3,2},{5,4},{6,5},{7,6},{9,8},{10,9},{11,10},{13,12},{... | collective-permute-start | bytes 393224 | tf_op jit(solution)/shard_map/ppermute | solution.py:23
  197.2 24.7 %collective-permute-start.1 = (f32[8,1,1,4096]{3,2,0,1:T(1,128)S(1)}, f32[8,1,1,4096]{3,2,0,1:T(1,128)S(1)}, u32[]{:S(2)}, u32[]{:S(2)}) collective-permute-start(f32[8,1,1,4096]{3,2,0,1:T(1,128)S(1)} %get-tuple-element.13), channel_id=1, source_target_pairs={{0,1},{1,2},{2,3},{4,5},{5,6},{6,7},{8,9},{9,10},{10,11},{12,13},{... | collective-permute-start | bytes 393224 | tf_op jit(solution)/shard_map/ppermute | solution.py:20
  203.3 19.9 %collective-permute-start = (f32[8,1,1,4096]{3,2,0,1:T(1,128)S(1)}, f32[8,1,1,4096]{3,2,0,1:T(1,128)S(1)}, u32[]{:S(2)}, u32[]{:S(2)}) collective-permute-start(f32[8,1,1,4096]{3,2,0,1:T(1,128)S(1)} %get-tuple-element.12), channel_id=1, source_target_pairs={{1,0},{2,1},{3,2},{5,4},{6,5},{7,6},{9,8},{10,9},{11,10},{13,12},{... | collective-permute-start | bytes 393224 | tf_op jit(solution)/shard_map/ppermute | solution.py:23
  206.4 24.7 %collective-permute-start.21 = (f32[8,1,1,4096]{3,2,0,1:T(1,128)S(1)}, f32[8,1,1,4096]{3,2,0,1:T(1,128)S(1)}, u32[]{:S(2)}, u32[]{:S(2)}) collective-permute-start(f32[8,1,1,4096]{3,2,0,1:T(1,128)S(1)} %get-tuple-element.23), channel_id=1, source_target_pairs={{0,1},{1,2},{2,3},{4,5},{5,6},{6,7},{8,9},{9,10},{10,11},{12,13},{... | collective-permute-start | bytes 393224 | tf_op jit(solution)/shard_map/ppermute | solution.py:20
  212.7 19.7 %collective-permute-start.20 = (f32[8,1,1,4096]{3,2,0,1:T(1,128)S(1)}, f32[8,1,1,4096]{3,2,0,1:T(1,128)S(1)}, u32[]{:S(2)}, u32[]{:S(2)}) collective-permute-start(f32[8,1,1,4096]{3,2,0,1:T(1,128)S(1)} %get-tuple-element.22), channel_id=1, source_target_pairs={{1,0},{2,1},{3,2},{5,4},{6,5},{7,6},{9,8},{10,9},{11,10},{13,12},{... | collective-permute-start | bytes 393224 | tf_op jit(solution)/shard_map/ppermute | solution.py:23
  215.8 24.5 %collective-permute-start.15 = (f32[8,1,1,4096]{3,2,0,1:T(1,128)S(1)}, f32[8,1,1,4096]{3,2,0,1:T(1,128)S(1)}, u32[]{:S(2)}, u32[]{:S(2)}) collective-permute-start(f32[8,1,1,4096]{3,2,0,1:T(1,128)S(1)} %get-tuple-element.17), channel_id=1, source_target_pairs={{0,1},{1,2},{2,3},{4,5},{5,6},{6,7},{8,9},{9,10},{10,11},{12,13},{... | collective-permute-start | bytes 393224 | tf_op jit(solution)/shard_map/ppermute | solution.py:20
  221.9 19.7 %collective-permute-start.14 = (f32[8,1,1,4096]{3,2,0,1:T(1,128)S(1)}, f32[8,1,1,4096]{3,2,0,1:T(1,128)S(1)}, u32[]{:S(2)}, u32[]{:S(2)}) collective-permute-start(f32[8,1,1,4096]{3,2,0,1:T(1,128)S(1)} %get-tuple-element.16), channel_id=1, source_target_pairs={{1,0},{2,1},{3,2},{5,4},{6,5},{7,6},{9,8},{10,9},{11,10},{13,12},{... | collective-permute-start | bytes 393224 | tf_op jit(solution)/shard_map/ppermute | solution.py:23
  225.0 24.5 %collective-permute-start.3 = (f32[8,1,1,4096]{3,2,0,1:T(1,128)S(1)}, f32[8,1,1,4096]{3,2,0,1:T(1,128)S(1)}, u32[]{:S(2)}, u32[]{:S(2)}) collective-permute-start(f32[8,1,1,4096]{3,2,0,1:T(1,128)S(1)} %get-tuple-element.11), channel_id=1, source_target_pairs={{0,1},{1,2},{2,3},{4,5},{5,6},{6,7},{8,9},{9,10},{10,11},{12,13},{... | collective-permute-start | bytes 393224 | tf_op jit(solution)/shard_map/ppermute | solution.py:20
  231.1 19.7 %collective-permute-start.2 = (f32[8,1,1,4096]{3,2,0,1:T(1,128)S(1)}, f32[8,1,1,4096]{3,2,0,1:T(1,128)S(1)}, u32[]{:S(2)}, u32[]{:S(2)}) collective-permute-start(f32[8,1,1,4096]{3,2,0,1:T(1,128)S(1)} %get-tuple-element.10), channel_id=1, source_target_pairs={{1,0},{2,1},{3,2},{5,4},{6,5},{7,6},{9,8},{10,9},{11,10},{13,12},{... | collective-permute-start | bytes 393224 | tf_op jit(solution)/shard_map/ppermute | solution.py:23
  234.2 24.5 %collective-permute-start.23 = (f32[8,1,1,4096]{3,2,0,1:T(1,128)S(1)}, f32[8,1,1,4096]{3,2,0,1:T(1,128)S(1)}, u32[]{:S(2)}, u32[]{:S(2)}) collective-permute-start(f32[8,1,1,4096]{3,2,0,1:T(1,128)S(1)} %get-tuple-element.21), channel_id=1, source_target_pairs={{0,1},{1,2},{2,3},{4,5},{5,6},{6,7},{8,9},{9,10},{10,11},{12,13},{... | collective-permute-start | bytes 393224 | tf_op jit(solution)/shard_map/ppermute | solution.py:20
  240.3 20.1 %collective-permute-start.22 = (f32[8,1,1,4096]{3,2,0,1:T(1,128)S(1)}, f32[8,1,1,4096]{3,2,0,1:T(1,128)S(1)}, u32[]{:S(2)}, u32[]{:S(2)}) collective-permute-start(f32[8,1,1,4096]{3,2,0,1:T(1,128)S(1)} %get-tuple-element.20), channel_id=1, source_target_pairs={{1,0},{2,1},{3,2},{5,4},{6,5},{7,6},{9,8},{10,9},{11,10},{13,12},{... | collective-permute-start | bytes 393224 | tf_op jit(solution)/shard_map/ppermute | solution.py:23
  243.4 18.5 %collective-permute-start.17 = (f32[8,1,1,4096]{3,2,0,1:T(1,128)S(1)}, f32[8,1,1,4096]{3,2,0,1:T(1,128)S(1)}, u32[]{:S(2)}, u32[]{:S(2)}) collective-permute-start(f32[8,1,1,4096]{3,2,0,1:T(1,128)S(1)} %get-tuple-element.15), channel_id=1, source_target_pairs={{0,1},{1,2},{2,3},{4,5},{5,6},{6,7},{8,9},{9,10},{10,11},{12,13},{... | collective-permute-start | bytes 393224 | tf_op jit(solution)/shard_map/ppermute | solution.py:20
  249.5 12.4 %collective-permute-start.16 = (f32[8,1,1,4096]{3,2,0,1:T(1,128)S(1)}, f32[8,1,1,4096]{3,2,0,1:T(1,128)S(1)}, u32[]{:S(2)}, u32[]{:S(2)}) collective-permute-start(f32[8,1,1,4096]{3,2,0,1:T(1,128)S(1)} %get-tuple-element.14), channel_id=1, source_target_pairs={{1,0},{2,1},{3,2},{5,4},{6,5},{7,6},{9,8},{10,9},{11,10},{13,12},{... | collective-permute-start | bytes 393224 | tf_op jit(solution)/shard_map/ppermute | solution.py:23
  252.6 10.8 %collective-permute-start.5 = (f32[8,1,1,4096]{3,2,0,1:T(1,128)S(1)}, f32[8,1,1,4096]{3,2,0,1:T(1,128)S(1)}, u32[]{:S(2)}, u32[]{:S(2)}) collective-permute-start(f32[8,1,1,4096]{3,2,0,1:T(1,128)S(1)} %get-tuple-element.9), channel_id=1, source_target_pairs={{0,1},{1,2},{2,3},{4,5},{5,6},{6,7},{8,9},{9,10},{10,11},{12,13},{... | collective-permute-start | bytes 393224 | tf_op jit(solution)/shard_map/ppermute | solution.py:20
  258.7 9.3 %collective-permute-start.4 = (f32[8,1,1,4096]{3,2,0,1:T(1,128)S(1)}, f32[8,1,1,4096]{3,2,0,1:T(1,128)S(1)}, u32[]{:S(2)}, u32[]{:S(2)}) collective-permute-start(f32[8,1,1,4096]{3,2,0,1:T(1,128)S(1)} %get-tuple-element.8), channel_id=1, source_target_pairs={{1,0},{2,1},{3,2},{5,4},{6,5},{7,6},{9,8},{10,9},{11,10},{13,12},{... | collective-permute-start | bytes 393224 | tf_op jit(solution)/shard_map/ppermute | solution.py:23
  332.3 273.0 %all-to-all-start.5 = ((f32[128,1,256]{2,1,0:T(1,128)}), f32[128,1,256]{2,1,0:T(1,128)S(1)}, u32[]{:S(2)}, u32[]{:S(2)}) async-start(f32[128,1,256]{2,1,0:T(1,128)} %reshape.303), calls=%async_computation.5 | async-start | bytes 262144 | tf_op jit(solution)/shard_map/all_to_all | solution.py:79
  338.2 266.0 %all-reduce.26.cloned.1.call-start = ((), (), s32[]{:S(2)}) async-start(), calls=%async_computation.6 | async-start | bytes 131072 | tf_op jit(solution)/shard_map/psum | solution.py:81
Sparse Core Ops, SparseCore 0:
  344.0 260.1 all-reduce.25
